TPU v7x, 32 devices: a whole 2x2x4 slice. The times are simulated.
32 devices in a mesh: seq: 4 (over y, x), batch: 8 (over z, core).
Axes of the slice: x: 2, y: 2, z: 4, core: 2. Of those that a mesh axis runs over, the one named last changes fastest.
Arguments:
- tokens: bfloat16 [64, 512, 768], P('batch', 'seq'), may hold values from -6 to 6
- values: float32 [64, 512], P('batch', 'seq'), may hold values from -4 to 4
- lengths: int32 [64], P('batch'), may hold values from 128 to 512, as said below
- merge: float32 [768], replicated, may hold values from -3 to 3
- w_query: bfloat16 [768, 768], replicated, may hold values from -0.21875 to 0.21875
- w_key: bfloat16 [768, 768], replicated, may hold values from -0.21875 to 0.21875
- w_value: bfloat16 [768, 768], replicated, may hold values from -0.21875 to 0.21875
- w_output: bfloat16 [768, 768], replicated, may hold values from -0.4375 to 0.4375
- b_query: float32 [768], replicated, may hold values from -3 to 3
- b_value: float32 [768], replicated, may hold values from -3 to 3
- b_output: float32 [768], replicated, may hold values from -3 to 3
- gain_one: float32 [768], replicated, may hold values from 0.5 to 1.5
- shift_one: float32 [768], replicated, may hold values from -2 to 2
- w_inner: bfloat16 [768, 3072], replicated, may hold values from -0.21875 to 0.21875
- b_inner: float32 [3072], replicated, may hold values from -3 to 3
- w_outer: bfloat16 [3072, 768], replicated, may hold values from -0.109375 to 0.109375
- b_outer: float32 [768], replicated, may hold values from -2 to 2
- gain_two: float32 [768], replicated, may hold values from 0.5 to 1.5
- shift_two: float32 [768], replicated, may hold values from -2 to 2
- cotangent: bfloat16 [64, 512, 768], P('batch', 'seq'), may hold values from -6 to 6
Outputs:
- layer_out: float32 [64, 512, 768], P('batch', 'seq')
- grad_tokens: float32 [64, 512, 768], P('batch', 'seq')
- grad_merge: float32 [768], P('batch')
- grad_w_query: float32 [768, 768], P('batch')
- grad_w_key: float32 [768, 768], P('batch')
- grad_w_value: float32 [768, 768], P('batch')
- grad_w_output: float32 [768, 768], P('batch')
- grad_b_query: float32 [768], P('batch')
- grad_b_value: float32 [768], P('batch')
- grad_b_output: float32 [768], P('batch')
- grad_gain_one: float32 [768], P('batch')
- grad_shift_one: float32 [768], P('batch')
- grad_w_inner: float32 [768, 3072], P('batch')
- grad_b_inner: float32 [3072], P('batch')
- grad_w_outer: float32 [3072, 768], P('batch')
- grad_b_outer: float32 [768], P('batch')
- grad_gain_two: float32 [768], P('batch')
- grad_shift_two: float32 [768], P('batch')
Inputs may be any that keep to these rules, and one draw needn't show every extreme that they name: `lengths`: in each aligned block of 8 rows (the rows of one index of batch) one row, drawn from the seed, has all 512 slots real.
All inputs are finite; a program needn't handle non-finite values.
Results may differ from a plain program's by a relative error of at most 0.033.
Values may be sent and summed in bfloat16 or wider, within the bound.
No kernel may reach another device: no remote copies, remote signals or barrier semaphores. Data moves between devices by JAX's collectives and lax.ppermute only.
A program may use at most 256 MiB of HBM per device.

v0:
```python
import jax
import jax.numpy as jnp
from jax import lax
from jax.sharding import PartitionSpec as P

H = 12
DH = 64


def matmul(left, right):
    return jnp.dot(left, right, preferred_element_type=jnp.float32)


def norm_forward(inputs, gain, shift):
    center = inputs - jnp.mean(inputs, axis=-1, keepdims=True)
    rstd = lax.rsqrt(jnp.mean(center * center, axis=-1, keepdims=True) + 1e-05)
    normal = center * rstd
    return (normal * gain + shift, normal, rstd)


def norm_backward(grad, normal, rstd):
    first = jnp.mean(grad, axis=-1, keepdims=True)
    second = jnp.mean(grad * normal, axis=-1, keepdims=True)
    return rstd * (grad - first - normal * second)


def exact_gelu(inner):
    return jax.nn.gelu(inner, approximate=False)


def body(
    tokens,
    values,
    lengths,
    merge,
    w_query,
    w_key,
    w_value,
    w_output,
    b_query,
    b_value,
    b_output,
    gain_one,
    shift_one,
    w_inner,
    b_inner,
    w_outer,
    b_outer,
    gain_two,
    shift_two,
    cotangent,
):
    rows, span, width = tokens.shape
    count = rows * span
    scale = 1.0 / DH**0.5
    flat_values = values.reshape(count, 1)
    merged = tokens.astype(jnp.float32).reshape(count, width) + flat_values * merge
    merged_low = merged.astype(jnp.bfloat16)
    query = (matmul(merged_low, w_query) + b_query).astype(jnp.bfloat16)
    key_low = matmul(merged_low, w_key).astype(jnp.bfloat16)
    value_low = (matmul(merged_low, w_value) + b_value).astype(jnp.bfloat16)
    keys_all, values_all = (
        lax.all_gather(key_low.reshape(rows, span, width), "seq", axis=1, tiled=True),
        lax.all_gather(value_low.reshape(rows, span, width), "seq", axis=1, tiled=True),
    )
    full = keys_all.shape[1]
    valid = jnp.arange(full, dtype=jnp.int32)[None, :] < lengths[:, None]
    query_heads = query.reshape(rows, span, H, DH)

    def scores_of(keys_whole):
        raw = (
            jnp.einsum(
                "rqhd,rkhd->rhqk",
                query_heads,
                keys_whole.reshape(rows, full, H, DH),
                preferred_element_type=jnp.float32,
            )
            * scale
        )
        return jnp.where(valid[:, None, None, :], raw, -1e30)

    scores = scores_of(keys_all)
    peak = jnp.max(scores, axis=-1, keepdims=True)
    expo = jnp.exp(scores - peak)
    total = jnp.sum(expo, axis=-1, keepdims=True)
    lse = peak + jnp.log(total)
    prob_low = (expo / total).astype(jnp.bfloat16)
    context = jnp.einsum(
        "rhqk,rkhd->rqhd",
        prob_low,
        values_all.reshape(rows, full, H, DH),
        preferred_element_type=jnp.float32,
    )
    context_low = context.reshape(count, width).astype(jnp.bfloat16)
    attended = merged + matmul(context_low, w_output) + b_output
    normed, normal_one, rstd_one = norm_forward(attended, gain_one, shift_one)
    normed_low = normed.astype(jnp.bfloat16)
    inner = matmul(normed_low, w_inner) + b_inner
    activated, gelu_pull = jax.vjp(exact_gelu, inner)
    activated_low = activated.astype(jnp.bfloat16)
    summed = normed + matmul(activated_low, w_outer) + b_outer
    result, normal_two, rstd_two = norm_forward(summed, gain_two, shift_two)
    layer_out = result.reshape(rows, span, width)
    upstream = cotangent.astype(jnp.float32).reshape(count, width)
    grad_gain_two = jnp.sum(upstream * normal_two, axis=0)
    grad_shift_two = jnp.sum(upstream, axis=0)
    d_summed = norm_backward(upstream * gain_two, normal_two, rstd_two)
    d_branch = d_summed.astype(jnp.bfloat16)
    grad_w_outer = matmul(activated_low.T, d_branch)
    grad_b_outer = jnp.sum(d_branch.astype(jnp.float32), axis=0)
    (d_inner_full,) = gelu_pull(matmul(d_branch, w_outer.T))
    d_inner = d_inner_full.astype(jnp.bfloat16)
    grad_w_inner = matmul(normed_low.T, d_inner)
    grad_b_inner = jnp.sum(d_inner.astype(jnp.float32), axis=0)
    d_normed = d_summed + matmul(d_inner, w_inner.T)
    grad_gain_one = jnp.sum(d_normed * normal_one, axis=0)
    grad_shift_one = jnp.sum(d_normed, axis=0)
    d_attended = norm_backward(d_normed * gain_one, normal_one, rstd_one)
    d_attn = d_attended.astype(jnp.bfloat16)
    grad_w_output = matmul(context_low.T, d_attn)
    grad_b_output = jnp.sum(d_attn.astype(jnp.float32), axis=0)
    d_context = matmul(d_attn, w_output.T).astype(jnp.bfloat16).reshape(rows, span, H, DH)
    keys_back, values_back = (keys_all, values_all)
    prob = jnp.exp(scores_of(keys_back) - lse)
    d_prob = jnp.einsum(
        "rqhd,rkhd->rhqk",
        d_context,
        values_back.reshape(rows, full, H, DH),
        preferred_element_type=jnp.float32,
    )
    delta = jnp.sum(prob * d_prob, axis=-1, keepdims=True)
    d_scores = (prob * (d_prob - delta)).astype(jnp.bfloat16)
    d_query = (
        jnp.einsum(
            "rhqk,rkhd->rqhd",
            d_scores,
            keys_back.reshape(rows, full, H, DH),
            preferred_element_type=jnp.float32,
        )
        * scale
    )
    prob_back = prob.astype(jnp.bfloat16)
    d_key_part = (
        jnp.einsum("rhqk,rqhd->rkhd", d_scores, query_heads, preferred_element_type=jnp.float32)
        * scale
    )
    d_value_part = jnp.einsum(
        "rhqk,rqhd->rkhd", prob_back, d_context, preferred_element_type=jnp.float32
    )
    d_key, d_value = (
        lax.psum_scatter(
            d_key_part.reshape(rows, full, width).astype(jnp.bfloat16),
            "seq",
            scatter_dimension=1,
            tiled=True,
        ).astype(jnp.float32),
        lax.psum_scatter(
            d_value_part.reshape(rows, full, width).astype(jnp.bfloat16),
            "seq",
            scatter_dimension=1,
            tiled=True,
        ).astype(jnp.float32),
    )
    d_query_low = d_query.reshape(count, width).astype(jnp.bfloat16)
    d_key_low = d_key.reshape(count, width).astype(jnp.bfloat16)
    d_value_low = d_value.reshape(count, width).astype(jnp.bfloat16)
    grad_w_query = matmul(merged_low.T, d_query_low)
    grad_b_query = jnp.sum(d_query_low.astype(jnp.float32), axis=0)
    grad_w_key = matmul(merged_low.T, d_key_low)
    grad_w_value = matmul(merged_low.T, d_value_low)
    grad_b_value = jnp.sum(d_value_low.astype(jnp.float32), axis=0)
    d_merged = (
        d_attended
        + matmul(d_query_low, w_query.T)
        + matmul(d_key_low, w_key.T)
        + matmul(d_value_low, w_value.T)
    )
    grad_merge = jnp.sum(d_merged * flat_values, axis=0)
    grad_tokens = d_merged.reshape(rows, span, width)
    all_parts = (
        lax.psum_scatter(grad_merge, "batch", scatter_dimension=0, tiled=True),
        lax.psum_scatter(grad_w_query, "batch", scatter_dimension=0, tiled=True),
        lax.psum_scatter(grad_w_key, "batch", scatter_dimension=0, tiled=True),
        lax.psum_scatter(grad_w_value, "batch", scatter_dimension=0, tiled=True),
        lax.psum_scatter(grad_w_output, "batch", scatter_dimension=0, tiled=True),
        lax.psum_scatter(grad_b_query, "batch", scatter_dimension=0, tiled=True),
        lax.psum_scatter(grad_b_value, "batch", scatter_dimension=0, tiled=True),
        lax.psum_scatter(grad_b_output, "batch", scatter_dimension=0, tiled=True),
        lax.psum_scatter(grad_gain_one, "batch", scatter_dimension=0, tiled=True),
        lax.psum_scatter(grad_shift_one, "batch", scatter_dimension=0, tiled=True),
        lax.psum_scatter(grad_w_inner, "batch", scatter_dimension=0, tiled=True),
        lax.psum_scatter(grad_b_inner, "batch", scatter_dimension=0, tiled=True),
        lax.psum_scatter(grad_w_outer, "batch", scatter_dimension=0, tiled=True),
        lax.psum_scatter(grad_b_outer, "batch", scatter_dimension=0, tiled=True),
        lax.psum_scatter(grad_gain_two, "batch", scatter_dimension=0, tiled=True),
        lax.psum_scatter(grad_shift_two, "batch", scatter_dimension=0, tiled=True),
    )
    all_parts = (
        lax.psum(all_parts[0].astype(jnp.bfloat16), "seq").astype(jnp.float32),
        lax.psum(all_parts[1].astype(jnp.bfloat16), "seq").astype(jnp.float32),
        lax.psum(all_parts[2].astype(jnp.bfloat16), "seq").astype(jnp.float32),
        lax.psum(all_parts[3].astype(jnp.bfloat16), "seq").astype(jnp.float32),
        lax.psum(all_parts[4].astype(jnp.bfloat16), "seq").astype(jnp.float32),
        lax.psum(all_parts[5].astype(jnp.bfloat16), "seq").astype(jnp.float32),
        lax.psum(all_parts[6].astype(jnp.bfloat16), "seq").astype(jnp.float32),
        lax.psum(all_parts[7].astype(jnp.bfloat16), "seq").astype(jnp.float32),
        lax.psum(all_parts[8].astype(jnp.bfloat16), "seq").astype(jnp.float32),
        lax.psum(all_parts[9].astype(jnp.bfloat16), "seq").astype(jnp.float32),
        lax.psum(all_parts[10].astype(jnp.bfloat16), "seq").astype(jnp.float32),
        lax.psum(all_parts[11].astype(jnp.bfloat16), "seq").astype(jnp.float32),
        lax.psum(all_parts[12].astype(jnp.bfloat16), "seq").astype(jnp.float32),
        lax.psum(all_parts[13].astype(jnp.bfloat16), "seq").astype(jnp.float32),
        lax.psum(all_parts[14].astype(jnp.bfloat16), "seq").astype(jnp.float32),
        lax.psum(all_parts[15].astype(jnp.bfloat16), "seq").astype(jnp.float32),
    )
    return (layer_out, grad_tokens) + tuple(all_parts)


def solution(mesh):
    in_specs = (
        P("batch", "seq", None),
        P("batch", "seq"),
        P("batch"),
        P(),
        P(),
        P(),
        P(),
        P(),
        P(),
        P(),
        P(),
        P(),
        P(),
        P(),
        P(),
        P(),
        P(),
        P(),
        P(),
        P("batch", "seq", None),
    )
    out_specs = (
        P("batch", "seq", None),
        P("batch", "seq", None),
        P("batch"),
        P("batch", None),
        P("batch", None),
        P("batch", None),
        P("batch", None),
        P("batch"),
        P("batch"),
        P("batch"),
        P("batch"),
        P("batch"),
        P("batch", None),
        P("batch"),
        P("batch", None),
        P("batch"),
        P("batch"),
        P("batch"),
    )
    return jax.shard_map(body, mesh=mesh, in_specs=in_specs, out_specs=out_specs, check_vma=False)
```

profile of v0, /device:TPU:0, one launch (start us, length us, event | category | flops | bytes accessed | tf_op | source)
XLA Modules:
  0.0 905.8 jit_solution(14554748021323202405)
XLA Ops:
  26.7 58.1 %all-gather.5.cloned.1.call-done = bf16[8,512,768]{2,1,0:T(8,128)(2,1)} async-done(((bf16[8,128,768]{2,1,0:T(8,128)(2,1)}), bf16[8,512,768]{2,1,0:T(8,128)(2,1)}) %all-gather.5.cloned.1.call-update) | async-done | bytes 6291472 | tf_op jit(solution)/shard_map/all_gather | solution.py:63
  93.5 12.9 %fusion.12 = (f32[8,12,128]{2,1,0:T(8,128)S(1)}, f32[8,12,128,512]{3,2,1,0:T(8,128)}) fusion(pred[8,512]{1,0:T(8,128)(4,1)S(1)} %iota_compare_fusion, bf16[8,512,12,64]{1,3,2,0:T(8,128)(2,1)} %bitcast.111, bf16[8,128,12,64]{1,0,3,2:T(8,128)(2,1)S(1)} %bitcast.116), kind=kOutput, calls=%fused_computation.30 | convolution fusion | flops 824168448 | bytes 33083392 | tf_op jit(solution)/shard_map/rqhd,rkhd->rhqk/dot_general | solution.py:72
  106.4 11.5 %fusion = f32[8,12,128]{2,1,0:T(8,128)S(1)} fusion(f32[8,12,128]{2,1,0:T(8,128)S(1)} %get-tuple-element.59, f32[8,12,128,512]{3,2,1,0:T(8,128)} %get-tuple-element.60, pred[8,512]{1,0:T(8,128)(4,1)S(1)} %iota_compare_fusion), kind=kLoop, calls=%fused_computation.6 | loop fusion | flops 25153536 | bytes 25268224 | tf_op jit(solution)/shard_map/reduce_sum | solution.py:85
  118.5 39.0 %all-gather.3.cloned.1.call-done = bf16[8,512,768]{2,1,0:T(8,128)(2,1)} async-done(((bf16[8,128,768]{2,1,0:T(8,128)(2,1)}), bf16[8,512,768]{2,1,0:T(8,128)(2,1)}) %all-gather.3.cloned.1.call-update) | async-done | bytes 6291472 | tf_op jit(solution)/shard_map/all_gather | solution.py:64
  166.2 13.2 %fusion.34 = bf16[8,128,12,64]{1,3,2,0:T(8,128)(2,1)S(1)} fusion(bf16[8,512,12,64]{1,3,2,0:T(8,128)(2,1)} %bitcast.114, f32[8,12,128]{2,1,0:T(8,128)S(1)} %fusion, f32[8,12,128]{2,1,0:T(8,128)S(1)} %get-tuple-element.59, f32[8,12,128,512]{3,2,1,0:T(8,128)} %get-tuple-element.60, pred[8,512]{1,0:T(8,128)(4,1)S(1)} %iota_compare_fusion), kind=kOutput, calls=%fused_computation.82 | convolution fusion | flops 837550080 | bytes 33132544 | tf_op jit(solution)/shard_map/rhqk,rkhd->rqhd/dot_general | solution.py:88
  185.5 35.4 %multiply_convert_fusion.2 = (bf16[1024,3072]{1,0:T(8,128)(2,1)S(1)}, f32[1024,3072]{1,0:T(8,128)}, f32[1024,3072]{1,0:T(8,128)}) fusion(f32[3072]{0:T(1024)S(1)} %copy-done.45, bf16[768,3072]{1,0:T(8,128)(2,1)S(1)} %bitcast.139, f32[1024,768]{1,0:T(8,128)S(1)} %get-tuple-element.62, f32[768]{0:T(1024)S(1)} %copy-done.29, f32[768]{0:T(1024)S(1)} %copy-done.28, ...), kind=kOutput, calls=%fused_computation.15 | convolution fusion | flops 5043388416 | bytes 39348224 | tf_op jit(solution)/shard_map/dot_general | solution.py:11
  233.6 18.9 %convert_reduce_fusion = (f32[3072]{0:T(1024)S(1)}, bf16[1024,3072]{1,0:T(8,128)(2,1)}) fusion(f32[1024,3072]{1,0:T(8,128)} %get-tuple-element.57, bf16[3072,768]{1,0:T(8,128)(2,1)} %param.35, f32[1024,768]{1,0:T(8,128)} %get-tuple-element.53, f32[1024,3072]{1,0:T(8,128)} %get-tuple-element.63, f32[3072]{0:T(1024)S(1)} %copy-done.45), kind=kOutput, calls=%fused_computation.11 | convolution fusion | flops 4886098944 | bytes 39346176 | tf_op jit(solution)/shard_map/dot_general | solution.py:11
  252.5 10.1 %multiply_reduce_fusion.1 = (f32[768]{0:T(1024)S(1)}, f32[1024]{0:T(1024)S(1)}, f32[1024]{0:T(1024)S(1)}, f32[768]{0:T(1024)S(1)}, f32[1024,768]{1,0:T(8,128)S(1)}) fusion(f32[1024,768]{1,0:T(8,128)S(1)} %get-tuple-element.62, f32[1024]{0:T(1024)S(1)} %add_rsqrt_fusion.1, f32[1024]{0:T(1024)S(1)} %broadcast_multiply_fusion.4, f32[768]{0:T(1024)S(1)} %copy-done.28, ...), kind=kOutput, calls=%fused_computation.45 | convolution fusion | flops 4839698432 | bytes 20472832 | tf_op jit(solution)/shard_map/dot_general | solution.py:11
  270.3 23.9 %multiply_reduce_fusion = (f32[8,12,128]{2,1,0:T(8,128)S(1)}, f32[8,12,128,512]{3,2,1,0:T(8,128)}) fusion(f32[8,12,128]{2,1,0:T(8,128)S(1)} %copy-done.21, f32[8,12,128,512]{3,2,1,0:T(8,128)} %get-tuple-element.60, pred[8,512]{1,0:T(8,128)(4,1)S(1)} %copy-done.23, bf16[8,512,12,64]{1,3,2,0:T(8,128)(2,1)} %bitcast.115, bf16[8,128,12,64]{1,0,3,2:T(8,128)(2,1)S(1)} %bitcast.122), kind=kOutput, calls=%fused_computation.1 | convolution fusion | flops 836751360 | bytes 58298368 | tf_op jit(solution)/shard_map/rqhd,rkhd->rhqk/dot_general | solution.py:125
  294.1 17.1 %multiply_convert_fusion = bf16[8,12,128,512]{3,2,1,0:T(8,128)(2,1)S(1)} fusion(f32[8,12,128,512]{3,2,1,0:T(8,128)} %get-tuple-element.68, f32[8,12,128]{2,1,0:T(8,128)S(1)} %get-tuple-element.67, f32[8,12,128]{2,1,0:T(8,128)S(1)} %copy-done.21, f32[8,12,128,512]{3,2,1,0:T(8,128)} %get-tuple-element.60, pred[8,512]{1,0:T(8,128)(4,1)S(1)} %copy-done.23), kind=kLoop, calls=%fused_computation | loop fusion | flops 37748736 | bytes 63016960 | tf_op jit(solution)/shard_map/convert_element_type | solution.py:132
  327.9 14.6 %fusion.13 = bf16[8,12,64,512]{3,2,1,0:T(8,128)(2,1)} fusion(f32[8,12,128]{2,1,0:T(8,128)S(1)} %copy-done.21, f32[8,12,128,512]{3,2,1,0:T(8,128)} %get-tuple-element.60, pred[8,512]{1,0:T(8,128)(4,1)S(1)} %copy-done.23, bf16[8,128,12,64]{1,0,3,2:T(8,128)(2,1)S(1)} %bitcast.123), kind=kOutput, calls=%fused_computation.31 | convolution fusion | flops 833617920 | bytes 33083392 | tf_op jit(solution)/shard_map/rhqk,rqhd->rkhd/dot_general | solution.py:147
  353.9 11.1 %convert_reduce_fusion.5 = (f32[12,64]{1,0:T(8,128)S(1)}, bf16[8,128,12,64]{1,3,2,0:T(8,128)(2,1)S(1)}) fusion(bf16[8,512,12,64]{1,3,2,0:T(8,128)(2,1)} %bitcast.112, bf16[8,12,128,512]{3,2,1,0:T(8,128)(2,1)} %copy-done.1), kind=kOutput, calls=%fused_computation.48 | convolution fusion | flops 808451328 | bytes 20450304 | tf_op jit(solution)/shard_map/rhqk,rkhd->rqhd/dot_general | solution.py:134
  375.6 21.3 %reduce-scatter.9.cloned.1.call-done = bf16[8,128,768]{2,1,0:T(8,128)(2,1)} async-done(((bf16[8,512,768]{2,1,0:T(8,128)(2,1)}), bf16[8,128,768]{2,1,0:T(8,128)(2,1)}) %reduce-scatter.9.cloned.1.call-update) | async-done | bytes 1572880 | tf_op jit(solution)/shard_map/reduce_scatter | solution.py:151
  401.7 68.3 %reduce-scatter.11.cloned.1.call-done = bf16[8,128,768]{2,1,0:T(8,128)(2,1)} async-done(((bf16[8,512,768]{2,1,0:T(8,128)(2,1)}), bf16[8,128,768]{2,1,0:T(8,128)(2,1)}) %reduce-scatter.11.cloned.1.call-update) | async-done | bytes 1572880 | tf_op jit(solution)/shard_map/reduce_scatter | solution.py:157
  474.4 11.1 %fusion.54 = f32[768,3072]{1,0:T(8,128)} fusion(bf16[1024,3072]{1,0:T(8,128)(2,1)} %get-tuple-element.74, f32[1024,768]{1,0:T(8,128)} %copy-done.2, f32[768]{0:T(1024)S(1)} %copy-done.29, f32[768]{0:T(1024)S(1)} %copy-done.28, f32[1024]{0:T(1024)S(1)} %add_rsqrt_fusion.1, f32[1024]{0:T(1024)S(1)} %broadcast_multiply_fusion.4), kind=kOutput, calls=%fused_computation.122 | convolution fusion | flops 4835770368 | bytes 18888704 | tf_op jit(solution)/shard_map/dot_general | solution.py:11
  485.5 10.4 %fusion.47 = f32[3072,768]{1,0:T(8,128)} fusion(bf16[1024,3072]{1,0:T(8,128)(2,1)} %copy-done.51, f32[1024,768]{1,0:T(8,128)} %get-tuple-element.53), kind=kOutput, calls=%fused_computation.115 | convolution fusion | flops 4832624640 | bytes 18874368 | tf_op jit(solution)/shard_map/dot_general | solution.py:11
  496.2 12.5 %reduce-scatter.13.cloned.1.call-done = f32[96,768]{1,0:T(8,128)} async-done(((f32[768,768]{1,0:T(8,128)}), f32[96,768]{1,0:T(8,128)}) %reduce-scatter.13.cloned.1.call-update) | async-done | bytes 294928 | tf_op jit(solution)/shard_map/reduce_scatter | solution.py:182
  510.3 35.8 %reduce-scatter.19.cloned.1.call-done = f32[96,768]{1,0:T(8,128)} async-done(((f32[768,768]{1,0:T(8,128)}), f32[96,768]{1,0:T(8,128)}) %reduce-scatter.19.cloned.1.call-update) | async-done | bytes 294928 | tf_op jit(solution)/shard_map/reduce_scatter | solution.py:185
  547.7 36.2 %reduce-scatter.15.cloned.1.call-done = f32[96,768]{1,0:T(8,128)} async-done(((f32[768,768]{1,0:T(8,128)}), f32[96,768]{1,0:T(8,128)}) %reduce-scatter.15.cloned.1.call-update) | async-done | bytes 294928 | tf_op jit(solution)/shard_map/reduce_scatter | solution.py:183
  585.5 36.2 %reduce-scatter.17.cloned.1.call-done = f32[96,768]{1,0:T(8,128)} async-done(((f32[768,768]{1,0:T(8,128)}), f32[96,768]{1,0:T(8,128)}) %reduce-scatter.17.cloned.1.call-update) | async-done | bytes 294928 | tf_op jit(solution)/shard_map/reduce_scatter | solution.py:184
  623.4 99.5 %reduce-scatter.21.cloned.1.call-done = f32[96,3072]{1,0:T(8,128)} async-done(((f32[768,3072]{1,0:T(8,128)}), f32[96,3072]{1,0:T(8,128)}) %reduce-scatter.21.cloned.1.call-update) | async-done | bytes 1179664 | tf_op jit(solution)/shard_map/reduce_scatter | solution.py:191
  725.0 97.9 %reduce-scatter.23.cloned.1.call-done = f32[384,768]{1,0:T(8,128)} async-done(((f32[3072,768]{1,0:T(8,128)}), f32[384,768]{1,0:T(8,128)}) %reduce-scatter.23.cloned.1.call-update) | async-done | bytes 1179664 | tf_op jit(solution)/shard_map/reduce_scatter | solution.py:193
  836.3 26.4 %all-reduce.10 = (bf16[768]{0:T(1024)(128)(2,1)S(1)}, bf16[768]{0:T(1024)(128)(2,1)S(1)}, bf16[768]{0:T(1024)(128)(2,1)S(1)}, bf16[768]{0:T(1024)(128)(2,1)S(1)}...) all-reduce(f32[768]{0:T(1024)S(1)} %get-tuple-element.69, ...), channel_id=4, replica_groups=mesh['seq'=4,'batch'=8] {'batch'}, use_global_device_ids=true, to_apply=%region_14.15.clone | all-reduce | flops 9984 | bytes 59904
  878.6 13.1 %all-reduce.15.cloned.1.call-done = (bf16[96,768]{1,0:T(8,128)(2,1)}, bf16[96,768]{1,0:T(8,128)(2,1)}, bf16[96,768]{1,0:T(8,128)(2,1)}, bf16[96,768]{1,0:T(8,128...) async-done(((bf16[96,768]{1,0:T(8,128)(2,1)}, bf16[96,768]{1,0:T(8,128)(2,1)}, bf16[96,768]{1,0:T(8,128)(2,1)}, bf16[96,768]{1,0:T(8,128)(2,1)}, ...) | async-done | bytes 1769488 | tf_op jit(solution)/shard_map/psum | solution.py:200
  (213 shorter events, 155.4 us)
Async XLA Ops:
  7.2 173.6 %copy-start = (bf16[768,768]{1,0:T(8,128)(2,1)S(1)}, bf16[768,768]{1,0:T(8,128)(2,1)}, u32[]{:S(2)}) copy-start(bf16[768,768]{1,0:T(8,128)(2,1)} %param.27) | copy-start | bytes 3538948
  7.2 77.7 %all-gather.5.cloned.1.call-start = ((), (), s32[]{:S(2)}) async-start(), calls=%async_computation.9 | async-start | bytes 7864320 | tf_op jit(solution)/shard_map/all_gather | solution.py:63
  11.9 145.6 %all-gather.3.cloned.1.call-start = ((), (), s32[]{:S(2)}) async-start(), calls=%async_computation.8 | async-start | bytes 7864320 | tf_op jit(solution)/shard_map/all_gather | solution.py:64
  15.8 381.1 %reduce-scatter.9.cloned.1.call-start = ((), (), s32[]{:S(2)}) async-start(), calls=%async_computation.10 | async-start | bytes 7864320 | tf_op jit(solution)/shard_map/reduce_scatter | solution.py:151
  24.8 68.7 %copy-start.3 = (bf16[96,8,8,128]{3,2,1,0:T(8,128)(2,1)}, bf16[96,8,8,128]{3,2,1,0:T(8,128)(2,1)S(1)}, u32[]{:S(2)}) copy-start(bf16[96,8,8,128]{3,2,1,0:T(8,128)(2,1)S(1)} %copy.78) | copy-start | bytes 4718596
  24.9 141.3 %copy-start.22 = (pred[8,512]{1,0:T(8,128)(4,1)}, pred[8,512]{1,0:T(8,128)(4,1)S(1)}, u32[]{:S(2)}) copy-start(pred[8,512]{1,0:T(8,128)(4,1)S(1)} %iota_compare_fusion) | copy-start | bytes 12292
  180.9 40.0 %slice-start = ((s8[4718592]{0:T(1024)(128)(4,1)}), s8[4194304]{0:T(1024)(128)(4,1)S(1)}, s32[]{:S(2)}) async-start(s8[4718592]{0:T(1024)(128)(4,1)} %bitcast.136), calls=%async_computation.19 | async-start | bytes 8388608
  182.8 79.7 %copy-start.2 = (f32[1024,768]{1,0:T(8,128)}, f32[1024,768]{1,0:T(8,128)S(1)}, u32[]{:S(2)}) copy-start(f32[1024,768]{1,0:T(8,128)S(1)} %get-tuple-element.62) | copy-start | bytes 9437188
  185.5 35.5 %slice-start.1 = ((s8[4718592]{0:T(1024)(128)(4,1)}), s8[524288]{0:T(1024)(128)(4,1)S(1)}, s32[]{:S(2)}) async-start(s8[4718592]{0:T(1024)(128)(4,1)} %bitcast.136), calls=%async_computation.20 | async-start | bytes 1048576
  185.5 35.5 %copy-start.49 = (f32[768]{0:T(1024)S(1)}, f32[768]{0:T(1024)}, u32[]{:S(2)}) copy-start(f32[768]{0:T(1024)} %param.36) | copy-start | bytes 9220
  270.2 23.9 %copy-start.12 = (bf16[96,8,8,128]{3,2,1,0:T(8,128)(2,1)}, bf16[96,8,8,128]{3,2,1,0:T(8,128)(2,1)S(1)}, u32[]{:S(2)}) copy-start(bf16[96,8,8,128]{3,2,1,0:T(8,128)(2,1)S(1)} %copy.80) | copy-start | bytes 4718596
  294.1 17.1 %copy-start.4 = (bf16[96,8,8,128]{3,2,1,0:T(8,128)(2,1)S(1)}, bf16[96,8,8,128]{3,2,1,0:T(8,128)(2,1)}, u32[]{:S(2)}) copy-start(bf16[96,8,8,128]{3,2,1,0:T(8,128)(2,1)} %copy-done.3) | copy-start | bytes 4718596
  326.5 143.5 %reduce-scatter.11.cloned.1.call-start = ((), (), s32[]{:S(2)}) async-start(), calls=%async_computation.11 | async-start | bytes 7864320 | tf_op jit(solution)/shard_map/reduce_scatter | solution.py:157
  350.9 157.7 %reduce-scatter.13.cloned.1.call-start = ((), (), s32[]{:S(2)}) async-start(), calls=%async_computation.12 | async-start | bytes 2654208 | tf_op jit(solution)/shard_map/reduce_scatter | solution.py:182
  370.3 175.7 %reduce-scatter.19.cloned.1.call-start = ((), (), s32[]{:S(2)}) async-start(), calls=%async_computation.15 | async-start | bytes 2654208 | tf_op jit(solution)/shard_map/reduce_scatter | solution.py:185
  375.5 94.5 %copy-start.19 = (bf16[8,128,768]{2,1,0:T(8,128)(2,1)S(1)}, bf16[8,128,768]{2,1,0:T(8,128)(2,1)}, u32[]{:S(2)}) copy-start(bf16[8,128,768]{2,1,0:T(8,128)(2,1)} %add_convert_fusion.1) | copy-start | bytes 4718596
  375.5 208.4 %reduce-scatter.15.cloned.1.call-start = ((), (), s32[]{:S(2)}) async-start(), calls=%async_computation.13 | async-start | bytes 2654208 | tf_op jit(solution)/shard_map/reduce_scatter | solution.py:183
  401.7 220.1 %reduce-scatter.17.cloned.1.call-start = ((), (), s32[]{:S(2)}) async-start(), calls=%async_computation.14 | async-start | bytes 2654208 | tf_op jit(solution)/shard_map/reduce_scatter | solution.py:184
  474.3 248.6 %reduce-scatter.21.cloned.1.call-start = ((), (), s32[]{:S(2)}) async-start(), calls=%async_computation.16 | async-start | bytes 10616832 | tf_op jit(solution)/shard_map/reduce_scatter | solution.py:191
  485.5 337.5 %reduce-scatter.23.cloned.1.call-start = ((), (), s32[]{:S(2)}) async-start(), calls=%async_computation.17 | async-start | bytes 10616832 | tf_op jit(solution)/shard_map/reduce_scatter | solution.py:193
  495.9 395.8 %all-reduce.15.cloned.1.call-start = ((), (), s32[]{:S(2)}) async-start(), calls=%async_computation.18 | async-start | bytes 3538944 | tf_op jit(solution)/shard_map/psum | solution.py:200
  547.7 277.4 %copy-start.50 = (u32[32]{0:T(128)S(1)}, u32[32]{0:T(128)}, u32[]{:S(2)}) copy-start(u32[32]{0:T(128)} %constant.85) | copy-start | bytes 388
  547.7 279.4 %copy-start.15 = (bf16[8,128,12,64]{1,0,3,2:T(8,128)(2,1)S(1)}, bf16[8,128,12,64]{1,0,3,2:T(8,128)(2,1)}, u32[]{:S(2)}) copy-start(bf16[8,128,12,64]{1,0,3,2:T(8,128)(2,1)} %copy-done.14) | copy-start | bytes 4718596
  891.8 6.6 copy-start.24
  (43 other events, 120.3 us)
Sparse Core Ops, SparseCore 0:
  12.0 72.8 all-gather.4
  87.3 70.1 all-gather.2
  326.6 70.2 reduce-scatter.8
  399.7 70.2 reduce-scatter.10
  472.1 36.4 reduce-scatter.12
  510.8 35.2 reduce-scatter.18
  548.4 35.4 reduce-scatter.14
  586.2 35.5 reduce-scatter.16
  624.0 98.8 reduce-scatter.20
  725.0 97.8 reduce-scatter.22
  827.9 63.8 all-reduce.14
where the time goes:
time: 911 us; the launch traced here: 906 us
  waiting for transfers between devices  518 us (57%)
  matrix products  210 us (23%)
  other arithmetic  66.3 us (7%)
  local copies, waits for them, and re-layouts  58 us (6%)
  blocking collectives  36.4 us (4%)
  between operations  16 us (2%)
    dot_general x18, matrix products, matmul(): return jnp.dot(left, right, preferred_element_type=jnp.float32)  130 us
    reduce_scatter x1, waiting for transfers between devices, body(): lax.psum_scatter(grad_w_inner, 'batch', scatter_dimension=0, tiled=True)  99.5 us
    reduce_scatter x1, waiting for transfers between devices, body(): lax.psum_scatter(grad_w_outer, 'batch', scatter_dimension=0, tiled=True)  97.9 us
    reduce_scatter x1, waiting for transfers between devices, body(): lax.psum_scatter(d_value_part.reshape(rows, full, width).astype(jnp.bfloa...  68.3 us
    all_gather x1, waiting for transfers between devices, body(): lax.all_gather(key_low.reshape(rows, span, width), 'seq', axis=1, tiled=T...  58.1 us
    all_gather x1, waiting for transfers between devices, body(): lax.all_gather(value_low.reshape(rows, span, width), 'seq', axis=1, tiled...  39 us
    reduce_scatter x1, waiting for transfers between devices, body(): lax.psum_scatter(grad_w_value, 'batch', scatter_dimension=0, tiled=True)  36.2 us
    reduce_scatter x1, waiting for transfers between devices, body(): lax.psum_scatter(grad_w_key, 'batch', scatter_dimension=0, tiled=True)  36.2 us
  transfers between devices with their start and end apart: 11, of which 11 were waited for; matrix products, arithmetic and copies ran while one was open for 16% of the time, Pallas kernels for 0%

commit v1 on v0

v1 whole, which is shorter than its diff:
```python
import functools

import jax
import jax.numpy as jnp
from jax import lax
from jax.experimental import pallas as pl
from jax.experimental.pallas import tpu as pltpu
from jax.sharding import PartitionSpec as P

DH = 64
LOG2E = 1.4426950408889634
RSQRT2 = 0.7071067811865476
RSQRT2PI = 0.3989422804014327
EPS = 1e-05
bf16 = jnp.bfloat16
f32 = jnp.float32
NN = (((1,), (0,)), ((), ()))
NT = (((1,), (1,)), ((), ()))
TN = (((0,), (0,)), ((), ()))
Shape = jax.ShapeDtypeStruct
VM = pl.BlockSpec(memory_space=pltpu.VMEM)
SM = pl.BlockSpec(memory_space=pltpu.SMEM)
LIMIT = 60 * 1024 * 1024


def dot(left, right, dims=NN):
    return lax.dot_general(left, right, dims, preferred_element_type=f32)


def params(*semantics):
    return pltpu.CompilerParams(vmem_limit_bytes=LIMIT, dimension_semantics=semantics or None)


def whole(shape):
    return pl.BlockSpec(shape, lambda *_: (0,) * len(shape))


def row_sum(block):
    return jnp.sum(block, axis=0, keepdims=True)


def pack_kernel(parts, place_ref, lengths_ref, tokens_ref, values_ref, merge_ref, *outs):
    sends, value_sends, order_ref, own_ref = (
        outs[:parts],
        outs[parts : 2 * parts],
        outs[2 * parts],
        outs[2 * parts + 1],
    )
    rows = tokens_ref.shape[0]
    share = rows // parts
    me = place_ref[0]
    for i in range(rows):
        rank = jnp.int32(0)
        for j in range(rows):
            if j != i:
                ahead = lengths_ref[j] >= lengths_ref[i] if j < i else lengths_ref[j] > lengths_ref[i]
                rank = rank + ahead.astype(jnp.int32)
        turn = rank // parts
        spot = rank % parts
        owner = jnp.where(turn % 2 == 0, spot, parts - 1 - spot)
        order_ref[owner * share + turn] = jnp.int32(i)
    for r in range(share):
        own_ref[r] = lengths_ref[order_ref[me * share + r]]
    columns = values_ref[...].T
    lane = lax.broadcasted_iota(jnp.int32, columns.shape, 1)
    for d in range(parts):
        for r in range(share):
            row = order_ref[(me ^ d) * share + r]
            column = jnp.sum(jnp.where(lane == row, columns, 0.0), axis=1, keepdims=True)
            sends[d][r] = (tokens_ref[row].astype(f32) + column * merge_ref[...]).astype(bf16)
            value_sends[d][pl.ds(r, 1), :] = values_ref[pl.ds(row, 1), :]


def deal_kernel(parts, place_ref, order_ref, source_ref, *sends):
    share = source_ref.shape[0] // parts
    me = place_ref[0]
    for d in range(parts):
        for r in range(share):
            sends[d][r] = source_ref[order_ref[(me ^ d) * share + r]]


def undeal_kernel(parts, place_ref, order_ref, *refs):
    received, out_ref = refs[:parts], refs[parts]
    share = out_ref.shape[0] // parts
    me = place_ref[0]
    for d in range(parts):
        for r in range(share):
            out_ref[order_ref[(me ^ d) * share + r]] = received[d][r].astype(f32)


def attend(length, q_ref, k_ref, v_ref, put_context, lse_ref):
    span, width = q_ref.shape
    c = LOG2E / DH**0.5
    lane = lax.broadcasted_iota(jnp.int32, (1, 128), 1)
    low = lane < DH

    def branch(n):
        def pair(p, carry):
            sl = pl.ds(pl.multiple_of(p * 128, 128), 128)
            q, k, v = q_ref[:, sl], k_ref[:n, sl], v_ref[:n, sl]
            real = lax.broadcasted_iota(jnp.int32, (span, 128), 1) + (n - 128) < length
            found, sizes = [], []
            for h in range(2):
                mine = low if h == 0 else ~low
                s = dot(jnp.where(mine, q, jnp.zeros_like(q)), k, NT)
                tail = jnp.where(real, s[:, n - 128 :], -1e30)
                s = jnp.concatenate([s[:, : n - 128], tail], axis=1) if n > 128 else tail
                peak = jnp.max(s, axis=1, keepdims=True) * c
                e = jnp.exp2(s * c - peak)
                total = jnp.sum(e, axis=1, keepdims=True)
                found.append(dot(e.astype(bf16), jnp.where(mine, v, jnp.zeros_like(v))) / total)
                sizes.append(peak + jnp.log2(total))
            put_context(sl, (found[0] + found[1]).astype(bf16))
            kept = jnp.where(lane == 2 * p, sizes[0], lse_ref[...])
            lse_ref[...] = jnp.where(lane == 2 * p + 1, sizes[1], kept)
            return carry

        lse_ref[...] = jnp.zeros_like(lse_ref)
        lax.fori_loop(0, width // 128, pair, 0)

    blocks = (length + 127) // 128
    for b in range(1, span // 128 + 1):
        pl.when(blocks == b)(functools.partial(branch, 128 * b))


def attend_back(length, q_ref, k_ref, v_ref, ctx_ref, lse_ref, do_ref, put):
    span, width = q_ref.shape
    scale = 1.0 / DH**0.5
    c = LOG2E * scale
    lane = lax.broadcasted_iota(jnp.int32, (1, 128), 1)
    low = lane < DH

    def branch(n):
        def pair(p, carry):
            sl = pl.ds(pl.multiple_of(p * 128, 128), 128)
            q, k, v, do = q_ref[:, sl], k_ref[:n, sl], v_ref[:n, sl], do_ref[:, sl]
            real = lax.broadcasted_iota(jnp.int32, (span, 128), 1) + (n - 128) < length
            product = do.astype(f32) * ctx_ref[:, sl].astype(f32)
            sizes = lse_ref[...]
            dq = dk = dv = 0.0
            for h in range(2):
                mine = low if h == 0 else ~low
                qh = jnp.where(mine, q, jnp.zeros_like(q))
                doh = jnp.where(mine, do, jnp.zeros_like(do))
                kh = jnp.where(mine, k, jnp.zeros_like(k))
                delta = jnp.sum(jnp.where(mine, product, 0.0), axis=1, keepdims=True)
                lse = jnp.sum(jnp.where(lane == 2 * p + h, sizes, 0.0), axis=1, keepdims=True)
                prob = jnp.exp2(dot(qh, k, NT) * c - lse)
                tail = jnp.where(real, prob[:, n - 128 :], 0.0)
                prob = jnp.concatenate([prob[:, : n - 128], tail], axis=1) if n > 128 else tail
                ds = (prob * (dot(doh, v, NT) - delta)).astype(bf16)
                dq = dq + dot(ds, kh)
                dk = dk + dot(ds, qh, TN)
                dv = dv + dot(prob.astype(bf16), doh, TN)
            put(0, sl, 0, span, (dq * scale).astype(bf16))
            put(1, sl, 0, n, (dk * scale).astype(bf16))
            put(2, sl, 0, n, dv.astype(bf16))
            if n < span:
                blank = jnp.zeros((span - n, 128), bf16)
                put(1, sl, n, span, blank)
                put(2, sl, n, span, blank)
            return carry

        lax.fori_loop(0, width // 128, pair, 0)

    blocks = (length + 127) // 128
    for b in range(1, span // 128 + 1):
        pl.when(blocks == b)(functools.partial(branch, 128 * b))


def forward_kernel(
    parts, place_ref, own_ref, wq_ref, wk_ref, wv_ref, wo_ref, bq_ref, bv_ref, bo_ref, *refs
):
    pieces = refs[:parts]
    xc_ref, q_ref, k_ref, v_ref, lse_ref, hat_ref, rstd_ref = refs[parts:]
    me = place_ref[0]
    step = pieces[0].shape[1]
    for d in range(parts):
        xc_ref[1, pl.ds(pl.multiple_of((me ^ d) * step, step), step), :] = pieces[d][0]
    x = xc_ref[1]
    q_ref[...] = (dot(x, wq_ref[...]) + bq_ref[...]).astype(bf16)
    k_ref[...] = dot(x, wk_ref[...]).astype(bf16)
    v_ref[...] = (dot(x, wv_ref[...]) + bv_ref[...]).astype(bf16)

    def put(sl, block):
        xc_ref[0, :, sl] = block

    attend(own_ref[pl.program_id(0)], q_ref, k_ref, v_ref, put, lse_ref)
    a = xc_ref[1].astype(f32) + dot(xc_ref[0], wo_ref[...]) + bo_ref[...]
    center = a - jnp.mean(a, axis=1, keepdims=True)
    rstd = lax.rsqrt(jnp.mean(center * center, axis=1, keepdims=True) + EPS)
    hat_ref[...] = center * rstd
    rstd_ref[...] = jnp.broadcast_to(rstd, rstd_ref.shape)


def feed_kernel(
    parts,
    place_ref,
    hat_ref,
    gain_one_ref,
    shift_one_ref,
    wi_ref,
    bi_ref,
    wo_ref,
    bo_ref,
    gain_ref,
    shift_ref,
    *refs,
):
    cot = refs[:parts]
    act_ref, slope_ref, low_ref, branch_ref = refs[parts : parts + 4]
    outs = refs[parts + 4 : 2 * parts + 4]
    sums_ref, total_ref, cot_ref, out_ref = refs[2 * parts + 4 :]
    step = pl.program_id(0)
    count, width = total_ref.shape
    me = place_ref[0]
    share, slots = cot[0].shape[0], cot[0].shape[1]

    @pl.when(step == 0)
    def _():
        normed = hat_ref[...] * gain_one_ref[...] + shift_one_ref[...]
        low_ref[...] = normed.astype(bf16)
        total_ref[...] = normed + bo_ref[...]

    inner = dot(low_ref[...], wi_ref[...]) + bi_ref[...]
    phi = 0.5 + 0.5 * lax.erf(inner * RSQRT2)
    act = (inner * phi).astype(bf16)
    slope_ref[...] = (phi + inner * (jnp.exp(-0.5 * inner * inner) * RSQRT2PI)).astype(bf16)
    act_ref[...] = act
    total_ref[...] += dot(act, wo_ref[...])

    @pl.when(step == pl.num_programs(0) - 1)
    def _():
        for d in range(parts):
            for r in range(share):
                base = pl.multiple_of((r * parts + (me ^ d)) * slots, slots)
                cot_ref[pl.ds(base, slots), :] = cot[d][r]

        def block(i, carry):
            sl = pl.ds(pl.multiple_of(i * 128, 128), 128)
            a = total_ref[sl, :]
            center = a - jnp.mean(a, axis=1, keepdims=True)
            rstd = lax.rsqrt(jnp.mean(center * center, axis=1, keepdims=True) + EPS)
            hat = center * rstd
            out_ref[sl, :] = (hat * gain_ref[...] + shift_ref[...]).astype(bf16)
            g = cot_ref[sl, :].astype(f32)
            scaled = g * gain_ref[...]
            first = jnp.mean(scaled, axis=1, keepdims=True)
            second = jnp.mean(scaled * hat, axis=1, keepdims=True)
            back = rstd * (scaled - first - hat * second)
            total_ref[sl, :] = back
            low = back.astype(bf16)
            branch_ref[sl, :] = low
            return (
                carry[0] + row_sum(g * hat),
                carry[1] + row_sum(g),
                carry[2] + row_sum(low.astype(f32)),
            )

        blank = jnp.zeros((1, width), f32)
        sums = lax.fori_loop(0, count // 128, block, (blank, blank, blank))
        sums_ref[...] = jnp.concatenate(sums + (jnp.zeros((5, width), f32),), axis=0)
        for d in range(parts):
            for r in range(share):
                base = pl.multiple_of((r * parts + (me ^ d)) * slots, slots)
                outs[d][r] = out_ref[pl.ds(base, slots), :]


def feed_back_kernel(
    branch_ref,
    summed_ref,
    hat_ref,
    rstd_ref,
    slope_ref,
    wi_ref,
    wo_ref,
    gain_ref,
    inner_ref,
    bias_ref,
    attended_ref,
    low_ref,
    sums_ref,
    total_ref,
):
    step = pl.program_id(0)
    count, width = total_ref.shape
    inner = (dot(branch_ref[...], wo_ref[...], NT) * slope_ref[...].astype(f32)).astype(bf16)
    inner_ref[...] = inner
    bias_ref[...] = row_sum(inner.astype(f32))

    @pl.when(step == 0)
    def _():
        total_ref[...] = summed_ref[...]

    total_ref[...] += dot(inner, wi_ref[...], NT)

    @pl.when(step == pl.num_programs(0) - 1)
    def _():
        def block(i, carry):
            sl = pl.ds(pl.multiple_of(i * 128, 128), 128)
            g = total_ref[sl, :]
            hat = hat_ref[sl, :]
            scaled = g * gain_ref[...]
            first = jnp.mean(scaled, axis=1, keepdims=True)
            second = jnp.mean(scaled * hat, axis=1, keepdims=True)
            back = rstd_ref[sl, :1] * (scaled - first - hat * second)
            attended_ref[sl, :] = back
            low = back.astype(bf16)
            low_ref[sl, :] = low
            return (
                carry[0] + row_sum(g * hat),
                carry[1] + row_sum(g),
                carry[2] + row_sum(low.astype(f32)),
            )

        blank = jnp.zeros((1, width), f32)
        sums = lax.fori_loop(0, count // 128, block, (blank, blank, blank))
        sums_ref[...] = jnp.concatenate(sums + (jnp.zeros((5, width), f32),), axis=0)


def backward_kernel(
    parts,
    place_ref,
    own_ref,
    xc_ref,
    q_ref,
    k_ref,
    v_ref,
    lse_ref,
    low_ref,
    attended_ref,
    wq_ref,
    wk_ref,
    wv_ref,
    wo_ref,
    *refs,
):
    values = refs[:parts]
    grads_ref = refs[parts]
    outs = refs[parts + 1 : 2 * parts + 1]
    sums_ref, do_ref, value_ref = refs[2 * parts + 1 :]
    r = pl.program_id(0)
    me = place_ref[0]
    slots = outs[0].shape[1]
    do_ref[...] = dot(low_ref[...], wo_ref[...], NT).astype(bf16)
    grads_ref[0] = low_ref[...]

    def put(which, sl, start, stop, block):
        grads_ref[1 + which, start:stop, sl] = block

    attend_back(own_ref[r], q_ref, k_ref, v_ref, xc_ref.at[0], lse_ref, do_ref, put)
    for d in range(parts):
        base = pl.multiple_of((me ^ d) * slots, slots)
        value_ref[:, pl.ds(base, slots)] = jnp.broadcast_to(values[d][pl.ds(r, 1), :], (8, slots))
    dq, dk, dv = grads_ref[1], grads_ref[2], grads_ref[3]
    total = (
        attended_ref[...]
        + dot(dq, wq_ref[...], NT)
        + dot(dk, wk_ref[...], NT)
        + dot(dv, wv_ref[...], NT)
    )
    low = total.astype(bf16)
    attended_ref[...] = total
    for d in range(parts):
        base = pl.multiple_of((me ^ d) * slots, slots)
        outs[d][0] = attended_ref[pl.ds(base, slots), :].astype(bf16)
    weight = value_ref[...]
    high = weight.astype(bf16)
    rest = (weight - high.astype(f32)).astype(bf16)
    merge = (dot(high, low) + dot(rest, low))[:1]
    sums = jnp.concatenate(
        [
            row_sum(dq.astype(f32)),
            row_sum(dv.astype(f32)),
            merge,
            jnp.zeros((5, merge.shape[1]), f32),
        ],
        axis=0,
    )

    @pl.when(r == 0)
    def _():
        sums_ref[...] = sums

    @pl.when(r > 0)
    def _():
        sums_ref[...] += sums


def outer_grad_kernel(parts, place_ref, act_ref, branch_ref, keep_ref, send_ref):
    me, core = place_ref[0], place_ref[1]
    whole_grad = dot(act_ref[...], branch_ref[...], TN).astype(bf16)
    pairs, rows = keep_ref.shape[1], keep_ref.shape[2]
    for z in range(pairs):
        for unit in range(parts):
            base = (2 * z * parts + unit) * rows
            even = whole_grad[base : base + rows]
            odd = whole_grad[base + parts * rows : base + (parts + 1) * rows]
            keep_ref[unit ^ me, z] = jnp.where(core == 0, even, odd)
            send_ref[unit ^ me, z] = jnp.where(core == 0, odd, even)


def unit_grad_kernel(place_ref, left_ref, right_ref, keep_ref, send_ref):
    core = place_ref[1]
    left = left_ref[0] if len(left_ref.shape) == 3 else left_ref[...]
    right = right_ref[0] if len(right_ref.shape) == 3 else right_ref[...]
    whole_grad = dot(left, right, TN).astype(bf16)
    pairs, rows = keep_ref.shape[1], keep_ref.shape[2]
    for z in range(pairs):
        even = whole_grad[2 * z * rows : (2 * z + 1) * rows]
        odd = whole_grad[(2 * z + 1) * rows : (2 * z + 2) * rows]
        keep_ref[0, z] = jnp.where(core == 0, even, odd)
        send_ref[0, z] = jnp.where(core == 0, odd, even)


def swap(array, axis, size, distance):
    return lax.ppermute(array, axis, [(i, i ^ distance) for i in range(size)])


def add_low(first, *others):
    total = first.astype(f32)
    for other in others:
        total = total + other.astype(f32)
    return total.astype(bf16)


def halve(block, bit, size, distance):
    split = block.reshape((block.shape[0] // 2, 2) + block.shape[1:])
    send = lax.dynamic_index_in_dim(split, 1 - bit, 1, keepdims=False)
    keep = lax.dynamic_index_in_dim(split, bit, 1, keepdims=False)
    return keep, swap(send, "batch", size, distance)


def reduce_units(keep, send, me, place, parts, size):
    part = add_low(keep, swap(send, "batch", size, 1))
    block = add_low(part[0], *[swap(part[d], "seq", parts, d) for d in range(1, parts)])
    distance = 2
    while distance < size:
        bit = (place // distance) % 2
        block = add_low(*halve(block, bit, size, distance))
        distance *= 2
    block = block[0]
    pieces = [block] + [swap(block, "seq", parts, d) for d in range(1, parts)]
    stack = jnp.stack(pieces)
    return [
        lax.dynamic_index_in_dim(stack, me ^ unit, 0, keepdims=False).astype(f32)
        for unit in range(parts)
    ]


def reduce_vectors(block, place, parts, size):
    distance = 1
    while distance < size:
        bit = (place // distance) % 2
        keep, got = halve(block, bit, size, distance)
        block = keep + got
        distance *= 2
    distance = 1
    while distance < parts:
        block = block + swap(block, "seq", parts, distance)
        distance *= 2
    return block[0]


def body(
    parts,
    size,
    tokens,
    values,
    lengths,
    merge,
    w_query,
    w_key,
    w_value,
    w_output,
    b_query,
    b_value,
    b_output,
    gain_one,
    shift_one,
    w_inner,
    b_inner,
    w_outer,
    b_outer,
    gain_two,
    shift_two,
    cotangent,
):
    rows, slots, width = tokens.shape
    hidden = w_inner.shape[1]
    share = rows // parts
    span = slots * parts
    count = share * span
    me = lax.axis_index("seq")
    place = lax.axis_index("batch")
    spot = jnp.stack([me, place % 2]).astype(jnp.int32)
    line = lambda vector: vector.reshape(1, -1)
    piece = Shape((share, slots, width), bf16)

    packed = pl.pallas_call(
        functools.partial(pack_kernel, parts),
        in_specs=[SM, SM, VM, VM, VM],
        out_specs=[VM] * (2 * parts) + [SM, SM],
        out_shape=[piece] * parts
        + [Shape((share, slots), f32)] * parts
        + [Shape((rows,), jnp.int32), Shape((share,), jnp.int32)],
        compiler_params=params(),
        name="pack",
    )(spot, lengths, tokens, values, line(merge))
    order, own = packed[2 * parts :]

    def exchange(pieces):
        return [pieces[0]] + [swap(pieces[d], "seq", parts, d) for d in range(1, parts)]

    x_parts = exchange(packed[:parts])
    value_parts = exchange(packed[parts : 2 * parts])
    cot_parts = exchange(
        pl.pallas_call(
            functools.partial(deal_kernel, parts),
            in_specs=[SM, SM, VM],
            out_specs=[VM] * parts,
            out_shape=[piece] * parts,
            compiler_params=params(),
            name="deal",
        )(spot, order, cotangent)
    )

    by_row = pl.BlockSpec((span, width), lambda r: (r, 0))
    row_piece = pl.BlockSpec((1, slots, width), lambda r: (r, 0, 0))
    square = whole((width, width))
    vector = whole((1, width))
    thin = pl.BlockSpec((span, 128), lambda r: (r, 0))
    xc, query, key, value, lse, hat_one, rstd_one = pl.pallas_call(
        functools.partial(forward_kernel, parts),
        grid=(share,),
        in_specs=[SM, SM] + [square] * 4 + [vector] * 3 + [row_piece] * parts,
        out_specs=[pl.BlockSpec((2, span, width), lambda r: (0, r, 0))]
        + [by_row] * 3
        + [thin, by_row, thin],
        out_shape=[Shape((2, count, width), bf16)]
        + [Shape((count, width), bf16)] * 3
        + [Shape((count, 128), f32), Shape((count, width), f32), Shape((count, 128), f32)],
        compiler_params=params("arbitrary"),
        name="attention_forward",
    )(
        spot,
        own,
        w_query,
        w_key,
        w_value,
        w_output,
        line(b_query),
        line(b_value),
        line(b_output),
        *x_parts,
    )

    chunk = 512
    steps = hidden // chunk
    tall = whole((count, width))
    wi_spec = pl.BlockSpec((width, chunk), lambda i: (0, i))
    wo_spec = pl.BlockSpec((chunk, width), lambda i: (i, 0))
    bi_spec = pl.BlockSpec((1, chunk), lambda i: (0, i))
    mid = pl.BlockSpec((count, chunk), lambda i: (0, i))
    pieces_spec = whole((share, slots, width))
    fed = pl.pallas_call(
        functools.partial(feed_kernel, parts),
        grid=(steps,),
        in_specs=[SM, tall, vector, vector, wi_spec, bi_spec, wo_spec]
        + [vector] * 3
        + [pieces_spec] * parts,
        out_specs=[mid, mid, tall, tall] + [pieces_spec] * parts + [whole((8, width)), tall],
        out_shape=[Shape((count, hidden), bf16)] * 2
        + [Shape((count, width), bf16)] * 2
        + [piece] * parts
        + [Shape((8, width), f32), Shape((count, width), f32)],
        scratch_shapes=[pltpu.VMEM((count, width), bf16), pltpu.VMEM((count, width), bf16)],
        compiler_params=params("arbitrary"),
        name="feed_forward",
    )(
        spot,
        hat_one,
        line(gain_one),
        line(shift_one),
        w_inner,
        line(b_inner),
        w_outer,
        line(b_outer),
        line(gain_two),
        line(shift_two),
        *cot_parts,
    )
    act, slope, normed_low, d_branch = fed[:4]
    out_parts = fed[4 : 4 + parts]
    sums_two, d_summed = fed[4 + parts :]

    def undeal(pieces):
        return pl.pallas_call(
            functools.partial(undeal_kernel, parts),
            in_specs=[SM, SM] + [VM] * parts,
            out_specs=VM,
            out_shape=Shape((rows, slots, width), f32),
            compiler_params=params(),
            name="undeal",
        )(spot, order, *pieces)

    layer_out = undeal(exchange(out_parts))

    pairs = size // 2
    blk = width // size
    unit_shape = Shape((parts, pairs, blk, width), bf16)
    per_chunk = pairs * width // hidden
    outer_keep, outer_send = pl.pallas_call(
        functools.partial(outer_grad_kernel, parts),
        grid=(hidden // width,),
        in_specs=[SM, pl.BlockSpec((count, width), lambda i: (0, i)), tall],
        out_specs=[pl.BlockSpec((parts, per_chunk, blk, width), lambda i: (0, i, 0, 0))] * 2,
        out_shape=[unit_shape] * 2,
        compiler_params=params("arbitrary"),
        name="outer_grad",
    )(spot, act, d_branch)

    d_inner, inner_bias, d_attended, d_attn, sums_one = pl.pallas_call(
        feed_back_kernel,
        grid=(steps,),
        in_specs=[tall, tall, tall, whole((count, 128)), mid, wi_spec, wo_spec, vector],
        out_specs=[mid, bi_spec, tall, tall, whole((8, width))],
        out_shape=[
            Shape((count, hidden), bf16),
            Shape((1, hidden), f32),
            Shape((count, width), f32),
            Shape((count, width), bf16),
            Shape((8, width), f32),
        ],
        scratch_shapes=[pltpu.VMEM((count, width), f32)],
        compiler_params=params("arbitrary"),
        name="feed_backward",
    )(d_branch, d_summed, hat_one, rstd_one, slope, w_inner, w_outer, line(gain_one))

    def unit_grads(left, right, left_spec, right_spec, name):
        return pl.pallas_call(
            unit_grad_kernel,
            grid_spec=pltpu.PrefetchScalarGridSpec(
                num_scalar_prefetch=1,
                grid=(parts,),
                in_specs=[left_spec, right_spec],
                out_specs=[pl.BlockSpec((1, pairs, blk, width), lambda d, spot: (d, 0, 0, 0))] * 2,
            ),
            out_shape=[unit_shape] * 2,
            compiler_params=params("arbitrary"),
            name=name,
        )(spot, left, right)

    inner_keep, inner_send = unit_grads(
        normed_low,
        d_inner,
        pl.BlockSpec((count, width), lambda d, spot: (0, 0)),
        pl.BlockSpec((count, width), lambda d, spot: (0, d ^ spot[0])),
        "inner_grad",
    )

    small = whole((share, slots))
    back = pl.pallas_call(
        functools.partial(backward_kernel, parts),
        grid=(share,),
        in_specs=[
            SM,
            SM,
            pl.BlockSpec((1, span, width), lambda r: (0, r, 0)),
            by_row,
            by_row,
            by_row,
            thin,
            by_row,
            by_row,
        ]
        + [square] * 4
        + [small] * parts,
        out_specs=[pl.BlockSpec((4, span, width), lambda r: (0, r, 0))]
        + [row_piece] * parts
        + [whole((8, width))],
        out_shape=[Shape((4, count, width), bf16)] + [piece] * parts + [Shape((8, width), f32)],
        scratch_shapes=[pltpu.VMEM((span, width), bf16), pltpu.VMEM((8, span), f32)],
        compiler_params=params("arbitrary"),
        name="attention_backward",
    )(
        spot,
        own,
        xc,
        query,
        key,
        value,
        lse,
        d_attn,
        d_attended,
        w_query,
        w_key,
        w_value,
        w_output,
        *value_parts,
    )
    grads, token_parts, sums_zero = back[0], back[1 : 1 + parts], back[1 + parts]
    grad_tokens = undeal(exchange(token_parts))

    last_keep, last_send = unit_grads(
        xc,
        grads,
        pl.BlockSpec((1, count, width), lambda d, spot: (jnp.minimum(d ^ spot[0], 1), 0, 0)),
        pl.BlockSpec((1, count, width), lambda d, spot: (d ^ spot[0], 0, 0)),
        "square_grad",
    )

    outer_units = reduce_units(outer_keep, outer_send, me, place, parts, size)
    inner_units = reduce_units(inner_keep, inner_send, me, place, parts, size)
    last_units = reduce_units(last_keep, last_send, me, place, parts, size)

    nine = jnp.concatenate([sums_two[:3], sums_one[:3], sums_zero[:3]], axis=0)
    vectors = jnp.concatenate(
        [
            nine.reshape(9, size, blk).transpose(1, 0, 2).reshape(size, 9 * blk),
            inner_bias.reshape(size, hidden // size),
        ],
        axis=1,
    )
    vectors = reduce_vectors(vectors, place, parts, size)
    nine = [vectors[i * blk : (i + 1) * blk] for i in range(9)]
    grad_gain_two, grad_shift_two, grad_b_outer = nine[:3]
    grad_gain_one, grad_shift_one, grad_b_output = nine[3:6]
    grad_b_query, grad_b_value, grad_merge = nine[6:]
    return (
        layer_out,
        grad_tokens,
        grad_merge,
        last_units[1],
        last_units[2],
        last_units[3],
        last_units[0],
        grad_b_query,
        grad_b_value,
        grad_b_output,
        grad_gain_one,
        grad_shift_one,
        jnp.concatenate(inner_units, axis=1),
        vectors[9 * blk :],
        jnp.concatenate(outer_units, axis=0),
        grad_b_outer,
        grad_gain_two,
        grad_shift_two,
    )


def solution(mesh):
    parts, size = mesh.shape["seq"], mesh.shape["batch"]
    rowwise = P("batch", "seq", None)
    in_specs = (rowwise, P("batch", "seq"), P("batch")) + (P(),) * 16 + (rowwise,)
    matrix, vector = P("batch", None), P("batch")
    out_specs = (
        (rowwise, rowwise, vector)
        + (matrix,) * 4
        + (vector,) * 5
        + (matrix, vector, matrix)
        + (vector,) * 3
    )
    return jax.shard_map(
        functools.partial(body, parts, size),
        mesh=mesh,
        in_specs=in_specs,
        out_specs=out_specs,
        check_vma=False,
    )
```

time: 911 us -> 347 us (0.38)
  waiting for transfers between devices: 518 us -> 116 us
  matrix products: 210 us -> 0 us
  Pallas kernels: 0 us -> 146 us
  starting transfers between devices: 1.03 us -> 56.7 us
  other arithmetic: 66.3 us -> 13.9 us
  local copies, waits for them, and re-layouts: 58 us -> 12.5 us
  blocking collectives: 36.4 us -> 0 us
  between operations: 16 us -> 1.29 us
    reduce_scatter x8 -> x0, waiting for transfers between devices: 408 us -> none  [the longest x1 99.5 us: body(): lax.psum_scatter(grad_w_inner, 'batch', scatter_dimension=0, tiled=True)]
    dot_general x24 -> x0, matrix products: 210 us -> none  [the longest x18 130 us: matmul(): return jnp.dot(left, right, preferred_element_type=jnp.float32)]
    pallas_call x0 -> x11, Pallas kernels: none -> 146 us  [the longest x1 31.6 us: body(): pl.pallas_call(functools.partial(backward_kernel, parts), grid=(share,),...]
    ppermute x0 -> x47, waiting for transfers between devices: none -> 116 us  [swap(): return lax.ppermute(array, axis, [(i, i ^ distance) for i in range(size)])]
    all_gather x2 -> x0, waiting for transfers between devices: 97.1 us -> none  [the longest x1 58.1 us: body(): lax.all_gather(key_low.reshape(rows, span, width), 'seq', axis=1, tiled=T...]
    ppermute x0 -> x47, starting transfers between devices: none -> 56.7 us  [swap(): return lax.ppermute(array, axis, [(i, i ^ distance) for i in range(size)])]
    convert_element_type x25 -> x13, other arithmetic: 44 us -> 9.35 us  [the longest x12 8.31 us: add_low(): return total.astype(bf16)]
    unnamed x1 -> x0, blocking collectives: 26.4 us -> none
  transfers between devices with their start and end apart: 11 -> 47, of which waited for: 11 -> 23; matrix products, arithmetic and copies ran while one was open for 16% -> 5% of each run, Pallas kernels for 0% -> 32%
where the time goes in v1:
time: 347 us; the launch traced here: 346 us
  Pallas kernels  146 us (42%)
  waiting for transfers between devices  116 us (33%)
  starting transfers between devices  56.7 us (16%)
  other arithmetic  13.9 us (4%)
  local copies, waits for them, and re-layouts  12.5 us (4%)
    ppermute x47, waiting for transfers between devices, swap(): return lax.ppermute(array, axis, [(i, i ^ distance) for i in range(size)])  116 us
    ppermute x47, starting transfers between devices, swap(): return lax.ppermute(array, axis, [(i, i ^ distance) for i in range(size)])  56.7 us
    pallas_call x1, Pallas kernels, body(): pl.pallas_call(functools.partial(backward_kernel, parts), grid=(share,),...  31.6 us
    pallas_call x1, Pallas kernels, body(): pl.pallas_call(feed_back_kernel, grid=(steps,), in_specs=[tall, tall, tal...  25.2 us
    pallas_call x1, Pallas kernels, body(): pl.pallas_call(functools.partial(feed_kernel, parts), grid=(steps,), in_s...  24.5 us
    pallas_call x1, Pallas kernels, body(): pl.pallas_call(functools.partial(forward_kernel, parts), grid=(share,), i...  22.7 us
    pallas_call x2, Pallas kernels, unit_grads(): pl.pallas_call(unit_grad_kernel, grid_spec=pltpu.PrefetchScalarGridSpec(n...  19.9 us
    pallas_call x1, Pallas kernels, body(): pl.pallas_call(functools.partial(outer_grad_kernel, parts), grid=(hidden...  9.36 us
  transfers between devices with their start and end apart: 47, of which 23 were waited for; matrix products, arithmetic and copies ran while one was open for 5% of the time, Pallas kernels for 32%

profile of v1, /device:TPU:0, one launch (start us, length us, event | category | flops | bytes accessed | tf_op | source)
XLA Modules:
  0.0 345.6 jit_solution(9867957844678131244)
XLA Ops:
  2.6 3.0 pack.1
  5.6 3.0 collective-permute-start
  18.8 3.0 collective-permute-start.5
  31.5 22.7 %attention_forward.1 = (bf16[2,1024,768]{2,1,0:T(8,128)(2,1)}, bf16[1024,768]{1,0:T(8,128)(2,1)}, bf16[1024,768]{1,0:T(8,128)(2,1)}, bf16[1024,768]{1,0:T(8,128)...) custom-call(s32[2]{0:T(128)} %pad_add_fusion.place_ref, s32[2]{0:T(128)} %get-tuple-element.67.own_ref, ...), custom_call_target="tpu_custom_call" | custom-call | tf_op jit(solution)/shard_map/attention_forward/pallas_call | solution.py:533
  57.3 24.5 %feed_forward.1 = (bf16[1024,3072]{1,0:T(8,128)(2,1)}, bf16[1024,3072]{1,0:T(8,128)(2,1)}, bf16[1024,768]{1,0:T(8,128)(2,1)}, bf16[1024,768]{1,0:T(8,128)(2,1)},...) custom-call(s32[2]{0:T(128)} %pad_add_fusion.place_ref, ...), custom_call_target="tpu_custom_call" | custom-call | tf_op jit(solution)/shard_map/feed_forward/pallas_call | solution.py:566
  82.5 25.2 %feed_backward.1 = (bf16[1024,3072]{1,0:T(8,128)(2,1)}, f32[1,3072]{1,0:T(1,128)}, f32[1024,768]{1,0:T(8,128)}, bf16[1024,768]{1,0:T(8,128)(2,1)}, f32[8,768]{1,0:T(8,128)}) custom-call(bf16[1024,768]{1,0:T(8,128)(2,1)} %get-tuple-element.86.branch_ref, f32[1024,768]{1,0:T(8,128)} %get-tuple-element.87.summed_ref, f32[1024,768]{1,0:T(8,128)} %get-tuple-element.72.hat_ref, ...), custom_call_target="tpu_custom_call" | custom-call | tf_op jit(solution)/shard_map/feed_backward/pallas_call | solution.py:623
  110.2 31.6 %attention_backward.1 = (bf16[4,1024,768]{2,1,0:T(8,128)(2,1)}, bf16[2,128,768]{2,1,0:T(8,128)(2,1)}, bf16[2,128,768]{2,1,0:T(8,128)(2,1)}, bf16[2,128,768]{2,1,...) custom-call(s32[2]{0:T(128)} %pad_add_fusion.place_ref, s32[2]{0:T(128)} %get-tuple-element.67.own_ref, ...), custom_call_target="tpu_custom_call" | custom-call | tf_op jit(solution)/shard_map/attention_backward/pallas_call | solution.py:663
  143.0 9.9 %square_grad.1 = (bf16[4,4,96,768]{3,2,1,0:T(8,128)(2,1)}, bf16[4,4,96,768]{3,2,1,0:T(8,128)(2,1)}) custom-call(s32[2]{0:T(128)} %pad_add_fusion.place_ref, bf16[2,1024,768]{2,1,0:T(8,128)(2,1)} %get-tuple-element.81.xc_ref.left_ref, bf16[4,1024,768]{2,1,0:T(8,128)(2,1)} %get-tuple-element.104.right_ref), custom_call_target="tpu_custom_call" | custom-call | tf_op jit(solution)/shard_map/square_grad/pallas_call | solution.py:641
  156.3 9.4 %outer_grad.1 = (bf16[4,4,96,768]{3,2,1,0:T(8,128)(2,1)}, bf16[4,4,96,768]{3,2,1,0:T(8,128)(2,1)}) custom-call(s32[2]{0:T(128)} %pad_add_fusion.place_ref, bf16[1024,3072]{1,0:T(8,128)(2,1)} %get-tuple-element.111.act_ref, bf16[1024,768]{1,0:T(8,128)(2,1)} %get-tuple-element.86.branch_ref), custom_call_target="tpu_custom_call" | custom-call | tf_op jit(solution)/shard_map/outer_grad/pallas_call | solution.py:613
  170.7 6.8 %collective-permute-done.18 = f32[1,1248]{1,0:T(1,128)S(1)} collective-permute-done((f32[1,1248]{1,0:T(1,128)S(1)}, f32[1,1248]{1,0:T(1,128)S(1)}, u32[]{:S(2)}, u32[]{:S(2)}) %collective-permute-start.18) | collective-permute-done | bytes 5024 | tf_op jit(solution)/shard_map/ppermute | solution.py:417
  180.0 10.0 %inner_grad.1 = (bf16[4,4,96,768]{3,2,1,0:T(8,128)(2,1)}, bf16[4,4,96,768]{3,2,1,0:T(8,128)(2,1)}) custom-call(s32[2]{0:T(128)} %pad_add_fusion.place_ref, bf16[1024,768]{1,0:T(8,128)(2,1)} %get-tuple-element.107.left_ref, bf16[1024,3072]{1,0:T(8,128)(2,1)} %get-tuple-element.108.right_ref), custom_call_target="tpu_custom_call" | custom-call | tf_op jit(solution)/shard_map/inner_grad/pallas_call | solution.py:641
  191.7 11.2 %collective-permute-done.8.refs_3_ = bf16[2,128,768]{2,1,0:T(8,128)(2,1)S(1)} collective-permute-done((bf16[2,128,768]{2,1,0:T(8,128)(2,1)S(1)}, bf16[2,128,768]{2,1,0:T(8,128)(2,1)S(1)}, u32[]{:S(2)}, u32[]{:S(2)}) %collective-permute-start.8) | collective-permute-done | bytes 393248 | tf_op jit(solution)/shard_map/ppermute | solution.py:417
  203.0 6.5 %collective-permute-done.12.refs_1_ = bf16[2,128,768]{2,1,0:T(8,128)(2,1)S(1)} collective-permute-done((bf16[2,128,768]{2,1,0:T(8,128)(2,1)S(1)}, bf16[2,128,768]{2,1,0:T(8,128)(2,1)S(1)}, u32[]{:S(2)}, u32[]{:S(2)}) %collective-permute-start.12) | collective-permute-done | bytes 393248 | tf_op jit(solution)/shard_map/ppermute | solution.py:417
  213.2 3.2 undeal.2
  216.4 5.2 %collective-permute-done.13.refs_2_ = bf16[2,128,768]{2,1,0:T(8,128)(2,1)S(1)} collective-permute-done((bf16[2,128,768]{2,1,0:T(8,128)(2,1)S(1)}, bf16[2,128,768]{2,1,0:T(8,128)(2,1)S(1)}, u32[]{:S(2)}, u32[]{:S(2)}) %collective-permute-start.13) | collective-permute-done | bytes 393248 | tf_op jit(solution)/shard_map/ppermute | solution.py:417
  222.5 3.4 undeal.3
  239.7 5.0 %collective-permute-done.21 = bf16[4,96,768]{2,1,0:T(8,128)(2,1)S(1)} collective-permute-done((bf16[4,96,768]{2,1,0:T(8,128)(2,1)S(1)}, bf16[4,96,768]{2,1,0:T(8,128)(2,1)S(1)}, u32[]{:S(2)}, u32[]{:S(2)}) %collective-permute-start.21) | collective-permute-done | bytes 589856 | tf_op jit(solution)/shard_map/ppermute | solution.py:417
  246.2 12.0 %collective-permute-done.23 = bf16[4,96,768]{2,1,0:T(8,128)(2,1)S(1)} collective-permute-done((bf16[4,96,768]{2,1,0:T(8,128)(2,1)S(1)}, bf16[4,96,768]{2,1,0:T(8,128)(2,1)S(1)}, u32[]{:S(2)}, u32[]{:S(2)}) %collective-permute-start.23) | collective-permute-done | bytes 589856 | tf_op jit(solution)/shard_map/ppermute | solution.py:417
  260.6 9.5 %collective-permute-done.39 = bf16[4,96,768]{2,1,0:T(8,128)(2,1)S(1)} collective-permute-done((bf16[4,96,768]{2,1,0:T(8,128)(2,1)S(1)}, bf16[4,96,768]{2,1,0:T(8,128)(2,1)S(1)}, u32[]{:S(2)}, u32[]{:S(2)}) %collective-permute-start.39) | collective-permute-done | bytes 589856 | tf_op jit(solution)/shard_map/ppermute | solution.py:417
  271.7 11.8 %collective-permute-done.41 = bf16[4,96,768]{2,1,0:T(8,128)(2,1)S(1)} collective-permute-done((bf16[4,96,768]{2,1,0:T(8,128)(2,1)S(1)}, bf16[4,96,768]{2,1,0:T(8,128)(2,1)S(1)}, u32[]{:S(2)}, u32[]{:S(2)}) %collective-permute-start.41) | collective-permute-done | bytes 589856 | tf_op jit(solution)/shard_map/ppermute | solution.py:417
  286.4 9.0 %collective-permute-done.30 = bf16[4,96,768]{2,1,0:T(8,128)(2,1)S(1)} collective-permute-done((bf16[4,96,768]{2,1,0:T(8,128)(2,1)S(1)}, bf16[4,96,768]{2,1,0:T(8,128)(2,1)S(1)}, u32[]{:S(2)}, u32[]{:S(2)}) %collective-permute-start.30) | collective-permute-done | bytes 589856 | tf_op jit(solution)/shard_map/ppermute | solution.py:417
  295.4 11.3 %collective-permute-done.32 = bf16[4,96,768]{2,1,0:T(8,128)(2,1)S(1)} collective-permute-done((bf16[4,96,768]{2,1,0:T(8,128)(2,1)S(1)}, bf16[4,96,768]{2,1,0:T(8,128)(2,1)S(1)}, u32[]{:S(2)}, u32[]{:S(2)}) %collective-permute-start.32) | collective-permute-done | bytes 589856 | tf_op jit(solution)/shard_map/ppermute | solution.py:417
  312.2 6.6 %collective-permute-done.33 = bf16[2,96,768]{2,1,0:T(8,128)(2,1)S(1)} collective-permute-done((bf16[2,96,768]{2,1,0:T(8,128)(2,1)S(1)}, bf16[2,96,768]{2,1,0:T(8,128)(2,1)S(1)}, u32[]{:S(2)}, u32[]{:S(2)}) %collective-permute-start.33) | collective-permute-done | bytes 294944 | tf_op jit(solution)/shard_map/ppermute | solution.py:417
  320.4 5.1 %collective-permute-start.28 = (bf16[96,768]{1,0:T(8,128)(2,1)S(1)}, bf16[96,768]{1,0:T(8,128)(2,1)S(1)}, u32[]{:S(2)}, u32[]{:S(2)}) collective-permute-start(bf16[96,768]{1,0:T(8,128)(2,1)S(1)} %bitcast.133), channel_id=1, source_target_pairs={{0,24},{8,16},{16,8},{24,0},{1,25},{9,17},{17,9},{25,1},{2,26},{10... | collective-permute-start | bytes 442376 | tf_op jit(solution)/shard_map/ppermute | solution.py:417
  (214 shorter events, 95.2 us)
Async XLA Ops:
  8.7 20.7 %collective-permute-start.1 = (bf16[2,128,768]{2,1,0:T(8,128)(2,1)}, bf16[2,128,768]{2,1,0:T(8,128)(2,1)S(1)}, u32[]{:S(2)}, u32[]{:S(2)}) collective-permute-start(bf16[2,128,768]{2,1,0:T(8,128)(2,1)} %get-tuple-element.70), channel_id=1, source_target_pairs={{0,16},{8,24},{16,0},{24,8},{1,17},{9,25},{17,1},{25,9},{2,18},{10... | collective-permute-start | bytes 1179656 | tf_op jit(solution)/shard_map/ppermute | solution.py:417
  10.2 19.2 %collective-permute-start.2 = (bf16[2,128,768]{2,1,0:T(8,128)(2,1)}, bf16[2,128,768]{2,1,0:T(8,128)(2,1)S(1)}, u32[]{:S(2)}, u32[]{:S(2)}) collective-permute-start(bf16[2,128,768]{2,1,0:T(8,128)(2,1)} %get-tuple-element.71), channel_id=1, source_target_pairs={{0,24},{8,16},{16,8},{24,0},{1,25},{9,17},{17,9},{25,1},{2,26},{10... | collective-permute-start | bytes 1179656 | tf_op jit(solution)/shard_map/ppermute | solution.py:417
  12.9 41.3 %collective-permute-start.3 = (bf16[2,128,768]{2,1,0:T(8,128)(2,1)}, bf16[2,128,768]{2,1,0:T(8,128)(2,1)S(1)}, u32[]{:S(2)}, u32[]{:S(2)}) collective-permute-start(bf16[2,128,768]{2,1,0:T(8,128)(2,1)} %get-tuple-element.74), channel_id=1, source_target_pairs={{0,8},{8,0},{16,24},{24,16},{1,9},{9,1},{17,25},{25,17},{2,10},{10... | collective-permute-start | bytes 1179656 | tf_op jit(solution)/shard_map/ppermute | solution.py:417
  14.8 41.5 %collective-permute-start.4 = (bf16[2,128,768]{2,1,0:T(8,128)(2,1)}, bf16[2,128,768]{2,1,0:T(8,128)(2,1)S(1)}, u32[]{:S(2)}, u32[]{:S(2)}) collective-permute-start(bf16[2,128,768]{2,1,0:T(8,128)(2,1)} %get-tuple-element.75), channel_id=1, source_target_pairs={{0,16},{8,24},{16,0},{24,8},{1,17},{9,25},{17,1},{25,9},{2,18},{10... | collective-permute-start | bytes 1179656 | tf_op jit(solution)/shard_map/ppermute | solution.py:417
  18.8 37.6 %collective-permute-start.5 = (bf16[2,128,768]{2,1,0:T(8,128)(2,1)}, bf16[2,128,768]{2,1,0:T(8,128)(2,1)S(1)}, u32[]{:S(2)}, u32[]{:S(2)}) collective-permute-start(bf16[2,128,768]{2,1,0:T(8,128)(2,1)} %get-tuple-element.76), channel_id=1, source_target_pairs={{0,24},{8,16},{16,8},{24,0},{1,25},{9,17},{17,9},{25,1},{2,26},{10... | collective-permute-start | bytes 1179656 | tf_op jit(solution)/shard_map/ppermute | solution.py:417
  29.3 80.2 %collective-permute-start.9 = (f32[2,128]{1,0:T(2,128)S(1)}, f32[2,128]{1,0:T(2,128)S(1)}, u32[]{:S(2)}, u32[]{:S(2)}) collective-permute-start(f32[2,128]{1,0:T(2,128)S(1)} %copy-done.35), channel_id=1, source_target_pairs={{0,8},{8,0},{16,24},{24,16},{1,9},{9,1},{17,25},{25,17},{2,10},{10... | collective-permute-start | bytes 3080 | tf_op jit(solution)/shard_map/ppermute | solution.py:417
  29.4 80.2 %collective-permute-start.10 = (f32[2,128]{1,0:T(2,128)S(1)}, f32[2,128]{1,0:T(2,128)S(1)}, u32[]{:S(2)}, u32[]{:S(2)}) collective-permute-start(f32[2,128]{1,0:T(2,128)S(1)} %copy-done.34), channel_id=1, source_target_pairs={{0,16},{8,24},{16,0},{24,8},{1,17},{9,25},{17,1},{25,9},{2,18},{10... | collective-permute-start | bytes 3080 | tf_op jit(solution)/shard_map/ppermute | solution.py:417
  54.2 55.4 %collective-permute-start.11 = (f32[2,128]{1,0:T(2,128)S(1)}, f32[2,128]{1,0:T(2,128)S(1)}, u32[]{:S(2)}, u32[]{:S(2)}) collective-permute-start(f32[2,128]{1,0:T(2,128)S(1)} %copy-done.33), channel_id=1, source_target_pairs={{0,24},{8,16},{16,8},{24,0},{1,25},{9,17},{17,9},{25,1},{2,26},{10... | collective-permute-start | bytes 3080 | tf_op jit(solution)/shard_map/ppermute | solution.py:417
  152.8 73.1 %collective-permute-start.20 = (bf16[4,4,96,768]{3,2,1,0:T(8,128)(2,1)}, bf16[4,4,96,768]{3,2,1,0:T(8,128)(2,1)}, u32[]{:S(2)}, u32[]{:S(2)}) collective-permute-start(bf16[4,4,96,768]{3,2,1,0:T(8,128)(2,1)} %get-tuple-element.106), channel_id=1, source_target_pairs={{0,1},{1,0},{2,3},{3,2},{4,5},{5,4},{6,7},{7,6},{8,9},{9,8},{10,11... | collective-permute-start | bytes 7077896 | tf_op jit(solution)/shard_map/ppermute | solution.py:417
  165.7 66.3 %collective-permute-start.38 = (bf16[4,4,96,768]{3,2,1,0:T(8,128)(2,1)}, bf16[4,4,96,768]{3,2,1,0:T(8,128)(2,1)}, u32[]{:S(2)}, u32[]{:S(2)}) collective-permute-start(bf16[4,4,96,768]{3,2,1,0:T(8,128)(2,1)} %get-tuple-element.113), channel_id=1, source_target_pairs={{0,1},{1,0},{2,3},{3,2},{4,5},{5,4},{6,7},{7,6},{8,9},{9,8},{10,11... | collective-permute-start | bytes 7077896 | tf_op jit(solution)/shard_map/ppermute | solution.py:417
  165.8 24.2 %collective-permute-start.6 = (bf16[2,128,768]{2,1,0:T(8,128)(2,1)S(1)}, bf16[2,128,768]{2,1,0:T(8,128)(2,1)S(1)}, u32[]{:S(2)}, u32[]{:S(2)}) collective-permute-start(bf16[2,128,768]{2,1,0:T(8,128)(2,1)S(1)} %copy-done.31), channel_id=1, source_target_pairs={{0,8},{8,0},{16,24},{24,16},{1,9},{9,1},{17,25},{25,17},{2,10},{10... | collective-permute-start | bytes 1179656 | tf_op jit(solution)/shard_map/ppermute | solution.py:417
  167.6 23.0 %collective-permute-start.7 = (bf16[2,128,768]{2,1,0:T(8,128)(2,1)S(1)}, bf16[2,128,768]{2,1,0:T(8,128)(2,1)S(1)}, u32[]{:S(2)}, u32[]{:S(2)}) collective-permute-start(bf16[2,128,768]{2,1,0:T(8,128)(2,1)S(1)} %copy-done.30), channel_id=1, source_target_pairs={{0,16},{8,24},{16,0},{24,8},{1,17},{9,25},{17,1},{25,9},{2,18},{10... | collective-permute-start | bytes 1179656 | tf_op jit(solution)/shard_map/ppermute | solution.py:417
  190.0 45.5 %collective-permute-start.29 = (bf16[4,4,96,768]{3,2,1,0:T(8,128)(2,1)}, bf16[4,4,96,768]{3,2,1,0:T(8,128)(2,1)}, u32[]{:S(2)}, u32[]{:S(2)}) collective-permute-start(bf16[4,4,96,768]{3,2,1,0:T(8,128)(2,1)} %get-tuple-element.110), channel_id=1, source_target_pairs={{0,1},{1,0},{2,3},{3,2},{4,5},{5,4},{6,7},{7,6},{8,9},{9,8},{10,11... | collective-permute-start | bytes 7077896 | tf_op jit(solution)/shard_map/ppermute | solution.py:417
  190.6 18.9 %collective-permute-start.12 = (bf16[2,128,768]{2,1,0:T(8,128)(2,1)S(1)}, bf16[2,128,768]{2,1,0:T(8,128)(2,1)S(1)}, u32[]{:S(2)}, u32[]{:S(2)}) collective-permute-start(bf16[2,128,768]{2,1,0:T(8,128)(2,1)S(1)} %copy-done.32), channel_id=1, source_target_pairs={{0,8},{8,0},{16,24},{24,16},{1,9},{9,1},{17,25},{25,17},{2,10},{10... | collective-permute-start | bytes 1179656 | tf_op jit(solution)/shard_map/ppermute | solution.py:417
  229.4 28.8 %collective-permute-start.23 = (bf16[4,96,768]{2,1,0:T(8,128)(2,1)S(1)}, bf16[4,96,768]{2,1,0:T(8,128)(2,1)S(1)}, u32[]{:S(2)}, u32[]{:S(2)}) collective-permute-start(bf16[4,96,768]{2,1,0:T(8,128)(2,1)S(1)} %get-tuple-element.121), channel_id=1, source_target_pairs={{0,24},{8,16},{16,8},{24,0},{1,25},{9,17},{17,9},{25,1},{2,26},{10... | collective-permute-start | bytes 1769480 | tf_op jit(solution)/shard_map/ppermute | solution.py:417
  231.3 28.9 %collective-permute-start.22 = (bf16[4,96,768]{2,1,0:T(8,128)(2,1)S(1)}, bf16[4,96,768]{2,1,0:T(8,128)(2,1)S(1)}, u32[]{:S(2)}, u32[]{:S(2)}) collective-permute-start(bf16[4,96,768]{2,1,0:T(8,128)(2,1)S(1)} %get-tuple-element.122), channel_id=1, source_target_pairs={{0,16},{8,24},{16,0},{24,8},{1,17},{9,25},{17,1},{25,9},{2,18},{10... | collective-permute-start | bytes 1769480 | tf_op jit(solution)/shard_map/ppermute | solution.py:417
  234.5 35.6 %collective-permute-start.39 = (bf16[4,96,768]{2,1,0:T(8,128)(2,1)S(1)}, bf16[4,96,768]{2,1,0:T(8,128)(2,1)S(1)}, u32[]{:S(2)}, u32[]{:S(2)}) collective-permute-start(bf16[4,96,768]{2,1,0:T(8,128)(2,1)S(1)} %get-tuple-element.114), channel_id=1, source_target_pairs={{0,8},{8,0},{16,24},{24,16},{1,9},{9,1},{17,25},{25,17},{2,10},{10... | collective-permute-start | bytes 1769480 | tf_op jit(solution)/shard_map/ppermute | solution.py:417
  235.5 48.0 %collective-permute-start.41 = (bf16[4,96,768]{2,1,0:T(8,128)(2,1)S(1)}, bf16[4,96,768]{2,1,0:T(8,128)(2,1)S(1)}, u32[]{:S(2)}, u32[]{:S(2)}) collective-permute-start(bf16[4,96,768]{2,1,0:T(8,128)(2,1)S(1)} %get-tuple-element.115), channel_id=1, source_target_pairs={{0,24},{8,16},{16,8},{24,0},{1,25},{9,17},{17,9},{25,1},{2,26},{10... | collective-permute-start | bytes 1769480 | tf_op jit(solution)/shard_map/ppermute | solution.py:417
  244.8 40.7 %collective-permute-start.40 = (bf16[4,96,768]{2,1,0:T(8,128)(2,1)S(1)}, bf16[4,96,768]{2,1,0:T(8,128)(2,1)S(1)}, u32[]{:S(2)}, u32[]{:S(2)}) collective-permute-start(bf16[4,96,768]{2,1,0:T(8,128)(2,1)S(1)} %get-tuple-element.116), channel_id=1, source_target_pairs={{0,16},{8,24},{16,0},{24,8},{1,17},{9,25},{17,1},{25,9},{2,18},{10... | collective-permute-start | bytes 1769480 | tf_op jit(solution)/shard_map/ppermute | solution.py:417
  258.2 37.2 %collective-permute-start.30 = (bf16[4,96,768]{2,1,0:T(8,128)(2,1)S(1)}, bf16[4,96,768]{2,1,0:T(8,128)(2,1)S(1)}, u32[]{:S(2)}, u32[]{:S(2)}) collective-permute-start(bf16[4,96,768]{2,1,0:T(8,128)(2,1)S(1)} %get-tuple-element.117), channel_id=1, source_target_pairs={{0,8},{8,0},{16,24},{24,16},{1,9},{9,1},{17,25},{25,17},{2,10},{10... | collective-permute-start | bytes 1769480 | tf_op jit(solution)/shard_map/ppermute | solution.py:417
  260.2 46.5 %collective-permute-start.32 = (bf16[4,96,768]{2,1,0:T(8,128)(2,1)S(1)}, bf16[4,96,768]{2,1,0:T(8,128)(2,1)S(1)}, u32[]{:S(2)}, u32[]{:S(2)}) collective-permute-start(bf16[4,96,768]{2,1,0:T(8,128)(2,1)S(1)} %get-tuple-element.118), channel_id=1, source_target_pairs={{0,24},{8,16},{16,8},{24,0},{1,25},{9,17},{17,9},{25,1},{2,26},{10... | collective-permute-start | bytes 1769480 | tf_op jit(solution)/shard_map/ppermute | solution.py:417
  270.1 37.9 %collective-permute-start.31 = (bf16[4,96,768]{2,1,0:T(8,128)(2,1)S(1)}, bf16[4,96,768]{2,1,0:T(8,128)(2,1)S(1)}, u32[]{:S(2)}, u32[]{:S(2)}) collective-permute-start(bf16[4,96,768]{2,1,0:T(8,128)(2,1)S(1)} %get-tuple-element.119), channel_id=1, source_target_pairs={{0,16},{8,24},{16,0},{24,8},{1,17},{9,25},{17,1},{25,9},{2,18},{10... | collective-permute-start | bytes 1769480 | tf_op jit(solution)/shard_map/ppermute | solution.py:417
  283.5 25.3 %collective-permute-start.24 = (bf16[2,96,768]{2,1,0:T(8,128)(2,1)S(1)}, bf16[2,96,768]{2,1,0:T(8,128)(2,1)S(1)}, u32[]{:S(2)}, u32[]{:S(2)}) collective-permute-start(bf16[2,96,768]{2,1,0:T(8,128)(2,1)S(1)} %dynamic-slice_bitcast_fusion.2), channel_id=1, source_target_pairs={{0,2},{1,3},{2,0},{3,1},{4,6},{5,7},{6,4},{7,5},{8,10},{9,11},{10,... | collective-permute-start | bytes 884744 | tf_op jit(solution)/shard_map/ppermute | solution.py:417
  285.8 25.8 %collective-permute-start.42 = (bf16[2,96,768]{2,1,0:T(8,128)(2,1)S(1)}, bf16[2,96,768]{2,1,0:T(8,128)(2,1)S(1)}, u32[]{:S(2)}, u32[]{:S(2)}) collective-permute-start(bf16[2,96,768]{2,1,0:T(8,128)(2,1)S(1)} %dynamic-slice_bitcast_fusion), channel_id=1, source_target_pairs={{0,2},{1,3},{2,0},{3,1},{4,6},{5,7},{6,4},{7,5},{8,10},{9,11},{10,... | collective-permute-start | bytes 884744 | tf_op jit(solution)/shard_map/ppermute | solution.py:417
  (59 other events, 707.9 us)
